TPU v7x, 512 devices: a whole 4x4x16 slice. The times are simulated.
512 devices in a mesh: dp: 32 (over y, x, core), tensor: 16 (over z).
Axes of the slice: x: 4, y: 4, z: 16, core: 2. Of those that a mesh axis runs over, the one named last changes fastest.
Arguments:
- attn_out: bfloat16 [3, 2048, 4096], P(None, 'dp', 'tensor'), may hold values from -6 to 6
- base_weight: bfloat16 [4096, 4096], P('tensor'), may hold values from -0.09375 to 0.09375
- store_a: bfloat16 [128, 4096, 128], P('dp', 'tensor'), may hold values from -0.09375 to 0.09375
- store_b: bfloat16 [128, 128, 4096], P('dp', None, 'tensor'), may hold values from -0.5 to 0.5
- adapter_lists: int32 [32, 16], P('dp'), may hold values from 0 to 127, as said below
- placement_map: int32 [128], replicated, may hold values from 0 to 127, as said below
- request_slot: int32 [2048], P('dp'), may hold values from 0 to 15
Outputs:
- projected: bfloat16 [3, 2048, 4096], P(None, 'dp', 'tensor')
Inputs may be any that keep to these rules, and one draw needn't show every extreme that they name: `adapter_lists`: each replica's 16 adapters are stored on 16 different indices of dp. `placement_map` is a permutation; adapter a's panels are row placement_map[a] of the stores, held by index placement_map[a] // 4 of dp.
All inputs are finite; a program needn't handle non-finite values.
Results may differ from a plain program's by a relative error of at most 0.001.
Values may be sent and summed in bfloat16 or wider, within the bound.
No kernel may reach another device: no remote copies, remote signals or barrier semaphores. Data moves between devices by JAX's collectives and lax.ppermute only.
A program may use at most 64 MiB of HBM per device.

v0:
```python
import jax
import jax.numpy as jnp
from jax import lax
from jax.sharding import PartitionSpec as P


def on_device(attn_out, base_weight, store_a, store_b, adapter_lists, placement_map, request_slot):
    replicas = lax.axis_size("dp")
    stored = store_a.shape[0]
    slot_count = adapter_lists.shape[1]
    rank_width = store_a.shape[2]
    requests = request_slot.shape[0]
    catalog = placement_map.shape[0]
    my_list = adapter_lists[0]
    matches = my_list[:, None] == jnp.arange(catalog, dtype=jnp.int32)[None, :]
    position = jnp.sum(jnp.where(matches, placement_map[None, :], 0), axis=1)
    holder = position // stored
    local_slot = position % stored
    devices = jnp.arange(replicas, dtype=jnp.int32)
    wanted = (
        jnp.sum(jnp.where(holder[None, :] == devices[:, None], local_slot[None, :] + 1, 0), axis=1)
        - 1
    )
    every_wish = lax.all_gather(wanted[None, :], "dp", axis=0, tiled=True)
    own_index = lax.axis_index("dp")
    asked_slot = lax.dynamic_index_in_dim(every_wish, own_index, 1, keepdims=False)
    picker = (asked_slot[:, None] == jnp.arange(stored, dtype=jnp.int32)[None, :]).astype(
        jnp.bfloat16
    )
    slot_hit = (request_slot[:, None] == jnp.arange(slot_count, dtype=jnp.int32)[None, :]).astype(
        jnp.float32
    )
    step_results = []
    for step_index in range(attn_out.shape[0]):
        send_a = jnp.einsum(
            "qn,nir->qir", picker, store_a, preferred_element_type=jnp.float32
        ).astype(jnp.bfloat16)
        send_b = jnp.einsum(
            "qn,nro->qro", picker, store_b, preferred_element_type=jnp.float32
        ).astype(jnp.bfloat16)
        recv_a = lax.all_to_all(send_a, "dp", split_axis=0, concat_axis=0, tiled=True)
        recv_b = lax.all_to_all(send_b, "dp", split_axis=0, concat_axis=0, tiled=True)
        slot_a = jnp.take(recv_a, holder, axis=0)
        slot_b = jnp.take(recv_b, holder, axis=0)
        fetch_stack_a = jnp.transpose(slot_a, (1, 0, 2)).reshape(
            slot_a.shape[1], slot_count * rank_width
        )
        fetch_stack_b = slot_b.reshape(slot_count * rank_width, slot_b.shape[2]).astype(jnp.float32)
        step_in = attn_out[step_index]
        base_output_sum = lax.psum_scatter(
            lax.dot_general(
                base_weight, step_in, (((0,), (1,)), ((), ())), preferred_element_type=jnp.float32
            ),
            "tensor",
            scatter_dimension=0,
            tiled=True,
        )
        every_slot = jnp.dot(step_in, fetch_stack_a, preferred_element_type=jnp.float32).reshape(
            requests, slot_count, rank_width
        )
        rank_part = jnp.sum(every_slot * slot_hit[:, :, None], axis=1)
        rank_reduce = lax.psum(rank_part, "tensor")
        spread = (slot_hit[:, :, None] * rank_reduce[:, None, :]).reshape(
            requests, slot_count * rank_width
        )
        low_rank_delta = jnp.dot(
            spread,
            fetch_stack_b,
            precision=lax.Precision.HIGHEST,
            preferred_element_type=jnp.float32,
        )
        step_results.append((base_output_sum.T + low_rank_delta).astype(jnp.bfloat16))
    return jnp.stack(step_results)


def solution(mesh):
    placed = (
        P(None, "dp", "tensor"),
        P("tensor", None),
        P("dp", "tensor", None),
        P("dp", None, "tensor"),
        P("dp", None),
        P(),
        P("dp"),
    )
    return jax.shard_map(
        on_device, mesh=mesh, in_specs=placed, out_specs=P(None, "dp", "tensor"), check_vma=False
    )
```

profile of v0, /device:TPU:8, one launch (start us, length us, event | category | flops | bytes accessed | tf_op | source)
XLA Modules:
  0.0 509.3 jit_solution(18405111244604827407)
XLA Ops:
  6.5 0.0 copy-start
  6.5 1.0 select_reduce_fusion.1
  7.6 0.1 select_reduce_fusion
  7.7 1.3 dynamic-slice
  9.6 0.1 add_dynamic-update-slice_fusion
  9.7 0.1 reshape.118
  9.8 111.4 %all-reduce.1 = s32[32,32]{1,0:T(8,128)S(1)} all-reduce(s32[32,32]{1,0:T(8,128)S(1)} %reshape.118), channel_id=2, replica_groups=mesh['dp'=32,'tensor'=16] {'dp'}, use_global_device_ids=true, to_apply=%add | all-reduce | flops 1024 | bytes 8192
  121.1 0.2 dynamic-slice_reduce_fusion
  121.3 1.7 convolution_convert_fusion.1
  123.1 2.1 copy.40
  125.2 0.0 copy-start.1
  125.2 22.7 %all-to-all-start = ((bf16[32,256,128]{2,1,0:T(8,128)(2,1)}), bf16[32,256,128]{2,1,0:T(8,128)(2,1)}, u32[]{:S(2)}, u32[]{:S(2)}) async-start(bf16[32,256,128]{2,1,0:T(8,128)(2,1)} %copy.40), calls=%async_computation.1 | async-start | bytes 4194304 | tf_op jit(solution)/shard_map/all_to_all | solution.py:41
  147.9 0.0 copy-start.3
  147.9 0.0 reduce-scatter.4.cloned.1.call-start
  148.0 0.0 copy-done
  148.0 0.0 copy-done.1
  148.0 1.5 fusion.30
  149.5 0.0 reduce-scatter.4.cloned.1.call-update
  149.5 0.0 all-reduce.5.cloned.1.call-start
  149.6 0.0 copy-done.3
  149.6 24.9 %all-to-all-done = bf16[32,256,128]{2,1,0:T(8,128)(2,1)} async-done(((bf16[32,256,128]{2,1,0:T(8,128)(2,1)}), bf16[32,256,128]{2,1,0:T(8,128)(2,1)}, u32[]{:S(2)}, u32[]{:S(2)}) %all-to-all-start) | async-done | bytes 2097184 | tf_op jit(solution)/shard_map/all_to_all | solution.py:41
  174.5 2.3 gather_fusion
  176.9 1.2 select_bitcast_fusion
  178.0 1.5 copy.41
  179.5 0.4 convolution_bitcast_fusion
  179.9 0.4 convolution_bitcast_fusion.1
  180.4 0.4 convolution_bitcast_fusion.2
  180.8 0.8 fusion.11
  181.6 0.0 all-reduce.5.cloned.1.call-update
  181.7 0.0 copy-start.2
  181.7 0.0 reduce-scatter.6.cloned.1.call-start
  181.7 1.5 fusion.27
  183.2 0.0 reduce-scatter.6.cloned.1.call-update
  183.3 0.0 copy-done.2
  183.3 0.8 convolution_convert_fusion
  184.0 2.5 copy.44
  186.5 8.1 %all-to-all-start.1 = ((bf16[32,128,256]{2,1,0:T(8,128)(2,1)}), bf16[32,128,256]{2,1,0:T(8,128)(2,1)}, u32[]{:S(2)}, u32[]{:S(2)}) async-start(bf16[32,128,256]{2,1,0:T(8,128)(2,1)} %copy.44), calls=%async_computation.2 | async-start | bytes 4194304 | tf_op jit(solution)/shard_map/all_to_all | solution.py:42
  194.7 0.0 reduce-scatter.8.cloned.1.call-start
  194.7 1.5 fusion.24
  196.2 0.0 reduce-scatter.8.cloned.1.call-update
  196.3 25.0 %all-to-all-done.1 = bf16[32,128,256]{2,1,0:T(8,128)(2,1)} async-done(((bf16[32,128,256]{2,1,0:T(8,128)(2,1)}), bf16[32,128,256]{2,1,0:T(8,128)(2,1)}, u32[]{:S(2)}, u32[]{:S(2)}) %all-to-all-start.1) | async-done | bytes 2097184 | tf_op jit(solution)/shard_map/all_to_all | solution.py:42
  221.3 2.2 gather_fusion.1
  223.5 2.1 reduce-scatter.4.cloned.1.call-done
  225.6 134.7 %all-reduce.5.cloned.1.call-done = (f32[64,128]{1,0:T(8,128)}, f32[64,128]{1,0:T(8,128)}, f32[64,128]{1,0:T(8,128)}) async-done(((f32[64,128]{1,0:T(8,128)}, f32[64,128]{1,0:T(8,128)}, f32[64,128]{1,0:T(8,128)}), (f32[64,128]{1,0:T(8,128)}, f32[64,128]{1,0:T(8,128)}, f32[64,128]{1,0:T(8,128)})) %all-reduce.5.cloned.1.call-update) | async-done | bytes 98320 | tf_op jit(solution)/shard_map/psum | solution.py:62
  360.3 0.0 copy-start.4
  360.3 1.6 fusion.6
  361.9 67.5 %reduce-scatter.6.cloned.1.call-done = f32[256,64]{0,1:T(8,128)} async-done(((f32[4096,64]{0,1:T(8,128)}), f32[256,64]{0,1:T(8,128)}) %reduce-scatter.6.cloned.1.call-update) | async-done | bytes 65552 | tf_op jit(solution)/shard_map/reduce_scatter | solution.py:50
  429.4 1.6 fusion.7
  431.0 69.5 %reduce-scatter.8.cloned.1.call-done = f32[256,64]{0,1:T(8,128)} async-done(((f32[4096,64]{0,1:T(8,128)}), f32[256,64]{0,1:T(8,128)}) %reduce-scatter.8.cloned.1.call-update) | async-done | bytes 65552 | tf_op jit(solution)/shard_map/reduce_scatter | solution.py:50
  500.5 0.0 copy-done.4
  500.5 1.6 fusion.8
  502.1 0.7 pad_maximum_fusion
  (6 shorter events, 0.0 us)
Async XLA Ops:
  6.5 141.5 %copy-start = (bf16[256,4096]{1,0:T(8,128)(2,1)S(1)}, bf16[256,4096]{1,0:T(8,128)(2,1)}, u32[]{:S(2)}) copy-start(bf16[256,4096]{1,0:T(8,128)(2,1)} %param.12) | copy-start | bytes 6291460
  125.2 22.8 %copy-start.1 = (bf16[3,64,256]{2,1,0:T(8,128)(2,1)S(1)}, bf16[3,64,256]{2,1,0:T(8,128)(2,1)}, u32[]{:S(2)}) copy-start(bf16[3,64,256]{2,1,0:T(8,128)(2,1)} %param.11) | copy-start | bytes 294916
  125.2 49.3 %all-to-all-start = ((bf16[32,256,128]{2,1,0:T(8,128)(2,1)}), bf16[32,256,128]{2,1,0:T(8,128)(2,1)}, u32[]{:S(2)}, u32[]{:S(2)}) async-start(bf16[32,256,128]{2,1,0:T(8,128)(2,1)} %copy.40), calls=%async_computation.1 | async-start | bytes 4194304 | tf_op jit(solution)/shard_map/all_to_all | solution.py:41
  147.9 1.6 copy-start.3
  147.9 77.7 %reduce-scatter.4.cloned.1.call-start = ((), (), s32[]{:S(2)}) async-start(), calls=%async_computation.5 | async-start | bytes 1114112 | tf_op jit(solution)/shard_map/reduce_scatter | solution.py:50
  149.5 210.8 %all-reduce.5.cloned.1.call-start = ((), (), s32[]{:S(2)}) async-start(), calls=%async_computation.8 | async-start | bytes 196608 | tf_op jit(solution)/shard_map/psum | solution.py:62
  181.7 1.6 copy-start.2
  181.7 247.7 %reduce-scatter.6.cloned.1.call-start = ((), (), s32[]{:S(2)}) async-start(), calls=%async_computation.6 | async-start | bytes 1114112 | tf_op jit(solution)/shard_map/reduce_scatter | solution.py:50
  186.5 34.7 %all-to-all-start.1 = ((bf16[32,128,256]{2,1,0:T(8,128)(2,1)}), bf16[32,128,256]{2,1,0:T(8,128)(2,1)}, u32[]{:S(2)}, u32[]{:S(2)}) async-start(bf16[32,128,256]{2,1,0:T(8,128)(2,1)} %copy.44), calls=%async_computation.2 | async-start | bytes 4194304 | tf_op jit(solution)/shard_map/all_to_all | solution.py:42
  194.7 305.9 %reduce-scatter.8.cloned.1.call-start = ((), (), s32[]{:S(2)}) async-start(), calls=%async_computation.7 | async-start | bytes 1114112 | tf_op jit(solution)/shard_map/reduce_scatter | solution.py:50
  360.3 140.2 %copy-start.4 = (f32[64,128]{1,0:T(8,128)S(1)}, f32[64,128]{1,0:T(8,128)}, u32[]{:S(2)}) copy-start(f32[64,128]{1,0:T(8,128)} %get-tuple-element.10) | copy-start | bytes 98308
Sparse Core Ops, SparseCore 0:
  151.6 73.9 reduce-scatter.3
  228.3 131.9 all-reduce.4
  363.1 66.2 reduce-scatter.5
  432.3 68.1 reduce-scatter.7
where the time goes:
time: 510 us; the launch traced here: 509 us
  waiting for transfers between devices  324 us (64%)
  blocking collectives  111 us (22%)
  starting transfers between devices  31.1 us (6%)
  between operations  13.9 us (3%)
  matrix products  13.1 us (3%)
  local copies, waits for them, and re-layouts  12.2 us (2%)
    reduce_scatter x3, waiting for transfers between devices, on_device(): lax.psum_scatter(lax.dot_general(base_weight, step_in, (((0,), (1,)), (()...  139 us
    psum x1, waiting for transfers between devices, on_device(): rank_reduce = lax.psum(rank_part, 'tensor')  135 us
    unnamed x1, blocking collectives  111 us
    all_to_all x1, waiting for transfers between devices, on_device(): lax.all_to_all(send_b, 'dp', split_axis=0, concat_axis=0, tiled=True)  25 us
    all_to_all x1, waiting for transfers between devices, on_device(): lax.all_to_all(send_a, 'dp', split_axis=0, concat_axis=0, tiled=True)  24.9 us
    all_to_all x1, starting transfers between devices, on_device(): lax.all_to_all(send_a, 'dp', split_axis=0, concat_axis=0, tiled=True)  22.7 us
  transfers between devices with their start and end apart: 6, of which 6 were waited for; matrix products, arithmetic and copies ran while one was open for 4% of the time, Pallas kernels for 0%

commit v1 on v0

--- a/solution.py
+++ b/solution.py
@@ -59,7 +59,7 @@
             requests, slot_count, rank_width
         )
         rank_part = jnp.sum(every_slot * slot_hit[:, :, None], axis=1)
-        rank_reduce = lax.psum(rank_part, "tensor")
+        rank_reduce = jnp.sum(lax.all_gather(rank_part, "tensor"), axis=0)
         spread = (slot_hit[:, :, None] * rank_reduce[:, None, :]).reshape(
             requests, slot_count * rank_width
         )

time: 510 us -> 307 us (0.60)
  the two profiles are of different devices: /device:TPU:8 before, /device:TPU:10 now
where the time goes in v1:
time: 307 us; the launch traced here: 306 us
  blocking collectives  205 us (67%)
  starting transfers between devices  36.9 us (12%)
  waiting for transfers between devices  20.8 us (7%)
  between operations  14 us (5%)
  local copies, waits for them, and re-layouts  13.8 us (4%)
  matrix products  12.9 us (4%)
    unnamed x1, blocking collectives  106 us
    all_gather x3, blocking collectives, on_device(): rank_reduce = jnp.sum(lax.all_gather(rank_part, 'tensor'), axis=0)  98.9 us
    all_to_all x1, starting transfers between devices, on_device(): lax.all_to_all(send_a, 'dp', split_axis=0, concat_axis=0, tiled=True)  27.6 us
    all_to_all x1, waiting for transfers between devices, on_device(): lax.all_to_all(send_a, 'dp', split_axis=0, concat_axis=0, tiled=True)  20.7 us
    all_to_all x1, starting transfers between devices, on_device(): lax.all_to_all(send_b, 'dp', split_axis=0, concat_axis=0, tiled=True)  9.14 us
  transfers between devices with their start and end apart: 5, of which 1 were waited for; matrix products, arithmetic and copies ran while one was open for 8% of the time, Pallas kernels for 0%

profile of v1, /device:TPU:10, one launch (start us, length us, event | category | flops | bytes accessed | tf_op | source)
XLA Modules:
  0.0 306.1 jit_solution(10289947724386621342)
XLA Ops:
  6.5 0.0 copy-start
  6.5 0.0 copy-start.1
  6.5 0.0 reduce-scatter.4.cloned.1.call-start
  6.5 1.6 copy-done
  8.1 2.2 fusion.30
  10.3 0.0 reduce-scatter.4.cloned.1.call-update
  10.4 0.0 copy-start.5
  10.4 0.0 copy-start.6
  10.4 0.0 copy-start.2
  10.4 0.0 reduce-scatter.6.cloned.1.call-start
  10.5 0.0 copy-done.1
  10.5 1.5 fusion.27
  11.9 0.0 reduce-scatter.6.cloned.1.call-update
  12.0 0.0 copy-done.5
  12.0 0.0 copy-done.6
  12.0 0.2 select_reduce_fusion.1
  12.2 0.1 select_reduce_fusion
  12.3 1.3 dynamic-slice
  14.2 0.1 add_dynamic-update-slice_fusion
  14.4 0.1 reshape.118
  14.4 106.3 %all-reduce.1 = s32[32,32]{1,0:T(8,128)S(1)} all-reduce(s32[32,32]{1,0:T(8,128)S(1)} %reshape.118), channel_id=2, replica_groups=mesh['dp'=32,'tensor'=16] {'dp'}, use_global_device_ids=true, to_apply=%add | all-reduce | flops 1024 | bytes 8192
  120.7 0.2 dynamic-slice_reduce_fusion
  120.9 0.0 copy-done.2
  120.9 0.8 convolution_convert_fusion.1
  121.7 2.1 copy.40
  123.8 27.6 %all-to-all-start = ((bf16[32,256,128]{2,1,0:T(8,128)(2,1)}), bf16[32,256,128]{2,1,0:T(8,128)(2,1)}, u32[]{:S(2)}, u32[]{:S(2)}) async-start(bf16[32,256,128]{2,1,0:T(8,128)(2,1)} %copy.40), calls=%async_computation.1 | async-start | bytes 4194304 | tf_op jit(solution)/shard_map/all_to_all | solution.py:41
  151.5 0.0 copy-start.3
  151.5 0.0 reduce-scatter.8.cloned.1.call-start
  151.6 1.6 fusion.24
  153.1 0.0 reduce-scatter.8.cloned.1.call-update
  153.1 0.0 copy-done.3
  153.2 0.8 convolution_convert_fusion
  153.9 2.5 copy.44
  156.4 0.0 copy-start.4
  156.4 20.7 %all-to-all-done = bf16[32,256,128]{2,1,0:T(8,128)(2,1)} async-done(((bf16[32,256,128]{2,1,0:T(8,128)(2,1)}), bf16[32,256,128]{2,1,0:T(8,128)(2,1)}, u32[]{:S(2)}, u32[]{:S(2)}) %all-to-all-start) | async-done | bytes 2097184 | tf_op jit(solution)/shard_map/all_to_all | solution.py:41
  177.1 9.1 %all-to-all-start.1 = ((bf16[32,128,256]{2,1,0:T(8,128)(2,1)}), bf16[32,128,256]{2,1,0:T(8,128)(2,1)}, u32[]{:S(2)}, u32[]{:S(2)}) async-start(bf16[32,128,256]{2,1,0:T(8,128)(2,1)} %copy.44), calls=%async_computation.2 | async-start | bytes 4194304 | tf_op jit(solution)/shard_map/all_to_all | solution.py:42
  186.3 0.0 copy-done.4
  186.3 2.3 gather_fusion
  188.6 1.2 select_bitcast_fusion
  189.8 1.5 copy.41
  191.3 0.4 convolution_bitcast_fusion
  191.7 0.4 convolution_bitcast_fusion.1
  192.2 0.4 convolution_bitcast_fusion.2
  192.6 0.2 fusion.11
  192.8 38.2 %all-gather.1 = f32[1024,128]{1,0:T(8,128)S(1)} all-gather(f32[64,128]{1,0:T(8,128)S(1)} %get-tuple-element.6), channel_id=3, replica_groups=mesh['dp'=32,'tensor'=16] {'tensor'}, dimensions={0}, use_global_device_ids=true | all-gather | bytes 557056 | tf_op jit(solution)/shard_map/all_gather | solution.py:62
  231.0 29.5 %all-gather.2 = f32[1024,128]{1,0:T(8,128)S(1)} all-gather(f32[64,128]{1,0:T(8,128)S(1)} %get-tuple-element.8), channel_id=4, replica_groups=mesh['dp'=32,'tensor'=16] {'tensor'}, dimensions={0}, use_global_device_ids=true | all-gather | bytes 557056 | tf_op jit(solution)/shard_map/all_gather | solution.py:62
  260.5 31.2 %all-gather.3 = f32[1024,128]{1,0:T(8,128)S(1)} all-gather(f32[64,128]{1,0:T(8,128)S(1)} %get-tuple-element.9), channel_id=5, replica_groups=mesh['dp'=32,'tensor'=16] {'tensor'}, dimensions={0}, use_global_device_ids=true | all-gather | bytes 557056 | tf_op jit(solution)/shard_map/all_gather | solution.py:62
  291.8 0.0 all-to-all-done.1
  291.8 2.2 gather_fusion.1
  294.0 0.0 reduce-scatter.4.cloned.1.call-done
  294.1 1.6 fusion.6
  295.6 0.0 reduce-scatter.6.cloned.1.call-done
  295.7 1.6 fusion.7
  297.3 0.0 reduce-scatter.8.cloned.1.call-done
  297.3 1.6 fusion.8
  298.9 0.7 pad_maximum_fusion
  (9 shorter events, 0.1 us)
Async XLA Ops:
  6.5 1.6 copy-start
  6.5 3.9 %copy-start.1 = (bf16[3,64,256]{2,1,0:T(8,128)(2,1)S(1)}, bf16[3,64,256]{2,1,0:T(8,128)(2,1)}, u32[]{:S(2)}) copy-start(bf16[3,64,256]{2,1,0:T(8,128)(2,1)} %param.11) | copy-start | bytes 294916
  6.5 287.5 %reduce-scatter.4.cloned.1.call-start = ((), (), s32[]{:S(2)}) async-start(), calls=%async_computation.5 | async-start | bytes 1114112 | tf_op jit(solution)/shard_map/reduce_scatter | solution.py:50
  10.4 1.6 copy-start.5
  10.4 1.6 copy-start.6
  10.4 110.5 %copy-start.2 = (bf16[4,256,128]{2,1,0:T(8,128)(2,1)S(1)}, bf16[4,256,128]{2,1,0:T(8,128)(2,1)}, u32[]{:S(2)}) copy-start(bf16[4,256,128]{2,1,0:T(8,128)(2,1)} %param.13) | copy-start | bytes 786436
  10.4 285.3 %reduce-scatter.6.cloned.1.call-start = ((), (), s32[]{:S(2)}) async-start(), calls=%async_computation.6 | async-start | bytes 1114112 | tf_op jit(solution)/shard_map/reduce_scatter | solution.py:50
  123.8 53.2 %all-to-all-start = ((bf16[32,256,128]{2,1,0:T(8,128)(2,1)}), bf16[32,256,128]{2,1,0:T(8,128)(2,1)}, u32[]{:S(2)}, u32[]{:S(2)}) async-start(bf16[32,256,128]{2,1,0:T(8,128)(2,1)} %copy.40), calls=%async_computation.1 | async-start | bytes 4194304 | tf_op jit(solution)/shard_map/all_to_all | solution.py:41
  151.5 1.6 copy-start.3
  151.5 145.8 %reduce-scatter.8.cloned.1.call-start = ((), (), s32[]{:S(2)}) async-start(), calls=%async_computation.7 | async-start | bytes 1114112 | tf_op jit(solution)/shard_map/reduce_scatter | solution.py:50
  156.4 29.8 %copy-start.4 = (s32[64]{0:T(128)S(1)}, s32[64]{0:T(128)}, u32[]{:S(2)}) copy-start(s32[64]{0:T(128)} %param.17) | copy-start | bytes 772
  177.1 114.7 %all-to-all-start.1 = ((bf16[32,128,256]{2,1,0:T(8,128)(2,1)}), bf16[32,128,256]{2,1,0:T(8,128)(2,1)}, u32[]{:S(2)}, u32[]{:S(2)}) async-start(bf16[32,128,256]{2,1,0:T(8,128)(2,1)} %copy.44), calls=%async_computation.2 | async-start | bytes 4194304 | tf_op jit(solution)/shard_map/all_to_all | solution.py:42
Sparse Core Ops, SparseCore 0:
  10.5 74.7 reduce-scatter.3
  88.3 68.1 reduce-scatter.5
  159.3 70.2 reduce-scatter.7
